TPU v7x, 128 devices: a whole 4x4x4 slice. The times are simulated.
128 devices in a mesh: gz: 32 (over y_hi, x, z), gy: 4 (over y_lo, core).
Axes of the slice: x: 4, y: 4 (y_hi: 2, y_lo: 2; y = y_hi * 2 + y_lo), z: 4, core: 2. Of those that a mesh axis runs over, the one named last changes fastest.
Arguments:
- state: float32 [9, 512, 64, 256], P(None, 'gz', 'gy'), may hold values from -6 to 6
- region: int32 [512, 64, 256], P('gz', 'gy'), may hold values from 0 to 7
- lame_table: float32 [8], replicated, may hold values from 0.5 to 2
- shear_table: float32 [8], replicated, may hold values from 0.3 to 1
- buoyancy_table: float32 [8], replicated, may hold values from 0.5 to 1.5
- face_block: int32 [32, 4, 32], P('gz', 'gy'), may hold values from 0 to 511, as said below
- face_owner: int32 [32, 4, 32], P('gz', 'gy'), may hold values from 0 to 31, as said below
- face_slot: int32 [32, 4, 32], P('gz', 'gy'), may hold values from 0 to 31, as said below
- joint_gain: float32 [32, 4, 16], P('gz', 'gy'), may hold values from 0.2 to 0.9
Outputs:
- final_state: float32 [9, 512, 64, 256], P(None, 'gz', 'gy')
- sensitivity: float32 [3, 512, 64, 256], P(None, 'gz', 'gy')
Inputs may be any that keep to these rules, and one draw needn't show every extreme that they name: `face_block`: within one device the blocks are distinct. `face_owner`: each device sends either none or exactly 2 faces to each owner; every owner receives 32 faces. `face_slot`: among the faces sent to one owner (same gy index) every slot 0 to 31 occurs exactly once.
All inputs are finite; a program needn't handle non-finite values.
Results may differ from a plain program's by a relative error of at most 0.000054.
Values sent between devices are 32-bit elements; how exact they have to be, the bound alone decides.
A program may use at most 64 MiB of HBM per device.

v0:
```python
import jax
import jax.numpy as jnp
from jax import lax
from jax.sharding import PartitionSpec as P

STEPS = 12
CAP = 2


c_near = 9.0 / 8.0
c_far = -1.0 / 24.0
time_step = 0.15
lane_width = 128


def with_halo(array, sides, width):
    for axis, dim in sides:
        devices, length = (lax.axis_size(axis), array.shape[dim])
        up = [(i, (i + 1) % devices) for i in range(devices - 1)]
        down = [(j, i) for i, j in up]
        last = lax.slice_in_dim(array, length - width, length, axis=dim)
        initial = lax.slice_in_dim(array, 0, width, axis=dim)
        before = lax.ppermute(last, axis, up)
        after = lax.ppermute(initial, axis, down)
        array = jnp.concatenate([before, array, after], axis=dim)
    return array


def difference(padded, axis, forward):
    length = padded.shape[axis] - 4

    def window(offset):
        return lax.slice_in_dim(padded, offset, offset + length, axis=axis)

    if forward:
        return c_near * (window(3) - window(2)) + c_far * (window(4) - window(1))
    return c_near * (window(2) - window(1)) + c_far * (window(3) - window(0))


def padded_along(field, axis):
    widths = [(0, 0), (0, 0), (0, 0)]
    widths[axis] = (2, 2)
    return jnp.pad(field, widths)


def velocity_update(vel, stress, buoy, y_rims, z_rims):
    force_x = (
        difference(padded_along(stress[0], 2), 2, True)
        + difference(y_rims[1], 1, False)
        + difference(z_rims[2], 0, False)
    )
    force_y = (
        difference(padded_along(stress[2], 2), 2, False)
        + difference(y_rims[0], 1, True)
        + difference(z_rims[0], 0, False)
    )
    force_z = (
        difference(padded_along(stress[5], 2), 2, False)
        + difference(y_rims[2], 1, False)
        + difference(z_rims[1], 0, True)
    )
    return jnp.stack(
        [
            vel[0] + time_step * buoy * force_x,
            vel[1] + time_step * buoy * force_y,
            vel[2] + time_step * buoy * force_z,
        ]
    )


def stress_update(vel, stress, lame, shear, y_rims, z_rims):
    strain_x = difference(padded_along(vel[0], 2), 2, False)
    strain_y = difference(y_rims[1], 1, False)
    strain_z = difference(z_rims[2], 0, False)
    dilation = strain_x + strain_y + strain_z
    new_xx = stress[0] + time_step * (lame * dilation + 2.0 * shear * strain_x)
    new_yy = stress[1] + time_step * (lame * dilation + 2.0 * shear * strain_y)
    new_zz = stress[4] + time_step * (lame * dilation + 2.0 * shear * strain_z)
    new_xy = stress[2] + time_step * shear * (
        difference(y_rims[0], 1, True) + difference(padded_along(vel[1], 2), 2, True)
    )
    new_yz = stress[3] + time_step * shear * (
        difference(z_rims[1], 0, True) + difference(y_rims[2], 1, True)
    )
    new_xz = stress[5] + time_step * shear * (
        difference(z_rims[0], 0, True) + difference(padded_along(vel[2], 2), 2, True)
    )
    return jnp.stack([new_xx, new_yy, new_xy, new_yz, new_zz, new_xz])


def lookup(region, table):
    total = jnp.zeros(region.shape, jnp.float32)
    for level in range(table.shape[0]):
        total = total + jnp.where(region == level, table[level], 0.0)
    return total


def exact_dot(left, right):
    return jnp.dot(left, right, precision=lax.Precision.HIGHEST, preferred_element_type=jnp.float32)


def per_device(
    state,
    region,
    lame_table,
    shear_table,
    buoyancy_table,
    face_block,
    face_owner,
    face_slot,
    joint_gain,
):
    lame = lookup(region, lame_table)
    shear = lookup(region, shear_table)
    buoy = lookup(region, buoyancy_table)
    groups = lax.axis_size("gz")
    blocks = face_block.reshape(-1)
    owners = face_owner.reshape(-1)
    slots = face_slot.reshape(-1)
    gains = joint_gain.reshape(-1)
    faces = blocks.shape[0]
    received_rows = groups * CAP
    face_ids = jnp.arange(faces, dtype=jnp.int32)
    earlier = (owners[None, :] == owners[:, None]) & (face_ids[None, :] < face_ids[:, None])
    ranking = jnp.sum(earlier.astype(jnp.int32), axis=1)
    position = owners * CAP + ranking
    send_match = jnp.arange(received_rows, dtype=jnp.int32)[:, None] == position[None, :]
    send_onehot = send_match.astype(jnp.float32)
    slot_buffer = jnp.sum(jnp.where(send_match, slots[None, :] + 1, 0), axis=1) - 1
    got_slots = lax.all_to_all(
        slot_buffer.reshape(groups, CAP), "gz", split_axis=0, concat_axis=0, tiled=True
    ).reshape(-1)
    recv_onehot = (face_ids[:, None] == got_slots[None, :]).astype(jnp.float32)

    def couple(vel):
        rows = vel.reshape(3, -1, lane_width)
        picked = jnp.take(rows, blocks, axis=1).transpose(1, 0, 2).reshape(faces, 3 * lane_width)
        outgoing = exact_dot(send_onehot, picked).reshape(groups, CAP, 3 * lane_width)
        incoming = lax.all_to_all(outgoing, "gz", split_axis=0, concat_axis=0, tiled=True).reshape(
            received_rows, 3 * lane_width
        )
        table = exact_dot(recv_onehot, incoming).reshape(faces // 2, 2, 3 * lane_width)
        slip = table[:, 0] - table[:, 1]
        traction = gains[:, None] * slip / jnp.sqrt(1.0 + slip * slip)
        halves = jnp.stack([-0.5 * traction, 0.5 * traction], axis=1).reshape(faces, 3 * lane_width)
        replies = exact_dot(recv_onehot.T, halves).reshape(groups, CAP, 3 * lane_width)
        answered = lax.all_to_all(replies, "gz", split_axis=0, concat_axis=0, tiled=True).reshape(
            received_rows, 3 * lane_width
        )
        delta = exact_dot(send_onehot.T, answered).reshape(faces, 3, lane_width).transpose(1, 0, 2)
        return rows.at[:, blocks].add(delta).reshape(vel.shape)

    def advance(step_index, carry):
        vel, stress, sens = carry
        full_stress = with_halo(stress, (("gz", 1), ("gy", 2)), 2)
        y_rims = full_stress[1:4, 2:-2]
        z_rims = full_stress[3:6, :, 2:-2]
        vel = velocity_update(vel, stress, buoy, y_rims, z_rims)
        vel = couple(vel)
        full_vel = with_halo(vel, (("gz", 1), ("gy", 2)), 2)
        vel_y = full_vel[:, 2:-2]
        vel_z = full_vel[:, :, 2:-2]
        stress = stress_update(vel, stress, lame, shear, vel_y, vel_z)
        sens = sens + time_step * vel
        return (vel, stress, sens)

    start_vel = state[0:3]
    start_stress = state[3:9]
    vel, stress, sens = lax.fori_loop(
        0, STEPS, advance, (start_vel, start_stress, jnp.zeros_like(start_vel))
    )
    return (jnp.concatenate([vel, stress], axis=0), sens)


def solution(mesh):
    return jax.shard_map(
        per_device,
        mesh=mesh,
        in_specs=(
            P(None, "gz", "gy", None),
            P("gz", "gy", None),
            P(),
            P(),
            P(),
            P("gz", "gy", None),
            P("gz", "gy", None),
            P("gz", "gy", None),
            P("gz", "gy", None),
        ),
        out_specs=(P(None, "gz", "gy", None), P(None, "gz", "gy", None)),
        check_vma=False,
    )
```

profile of v0, /device:TPU:1, one launch (start us, length us, event | category | flops | bytes accessed | tf_op | source)
XLA Modules:
  0.0 1368.6 jit_solution(13419401751885708874)
XLA Ops:
  8.6 6.2 select_add_fusion.1
  14.8 5.9 select_add_fusion.2
  20.7 6.1 select_add_fusion.3
  26.8 11.3 all-to-all-start.2
  39.8 6.9 all-to-all-done.2
  48.0 1318.9 %while.17 = (s32[]{:T(128)}, f32[3,16,16,256]{3,2,1,0:T(8,128)S(1)}, f32[6,16,16,256]{3,2,1,0:T(8,128)S(1)}, f32[3,16,16,256]{3,2,1,0:T(8,128)}, f32[16,16,256]{...) while((s32[]{:T(128)}, ...), condition=%wide.region_4.5_spmd.clone, body=%wide.region_2.4_spmd.clone.sunk | while | flops 48659744 | bytes 98147328 | solution.py:169
  53.5 3.2 collective-permute-done.1
  56.9 5.4 collective-permute-start.2
  81.9 20.6 %all_to_all.26 = f32[32,2,384]{2,1,0:T(2,128)S(1)} all-to-all(f32[32,2,384]{2,1,0:T(2,128)S(1)} %reshape.356), channel_id=1, replica_groups=mesh['gz'=32,'gy'=4] {'gz'}, dimensions={0} | all-to-all | bytes 196608 | tf_op jit(solution)/shard_map/while/body/eval_jaxpr/all_to_all | solution.py:139
  104.0 12.1 all_to_all.27
  132.1 4.8 collective-permute-start.6
  136.9 5.8 collective-permute-start.7
  158.8 3.3 collective-permute-done.1
  164.3 4.6 collective-permute-start.3
  186.2 26.4 %all_to_all.26 = f32[32,2,384]{2,1,0:T(2,128)S(1)} all-to-all(f32[32,2,384]{2,1,0:T(2,128)S(1)} %reshape.356), channel_id=1, replica_groups=mesh['gz'=32,'gy'=4] {'gz'}, dimensions={0} | all-to-all | bytes 196608 | tf_op jit(solution)/shard_map/while/body/eval_jaxpr/all_to_all | solution.py:139
  214.1 12.1 all_to_all.27
  245.9 6.9 collective-permute-start.7
  269.2 3.2 collective-permute-done.1
  274.5 4.7 collective-permute-start.3
  296.6 26.4 %all_to_all.26 = f32[32,2,384]{2,1,0:T(2,128)S(1)} all-to-all(f32[32,2,384]{2,1,0:T(2,128)S(1)} %reshape.356), channel_id=1, replica_groups=mesh['gz'=32,'gy'=4] {'gz'}, dimensions={0} | all-to-all | bytes 196608 | tf_op jit(solution)/shard_map/while/body/eval_jaxpr/all_to_all | solution.py:139
  324.5 12.1 all_to_all.27
  356.3 6.9 collective-permute-start.7
  379.6 3.2 collective-permute-done.1
  384.9 4.7 collective-permute-start.3
  406.9 26.4 %all_to_all.26 = f32[32,2,384]{2,1,0:T(2,128)S(1)} all-to-all(f32[32,2,384]{2,1,0:T(2,128)S(1)} %reshape.356), channel_id=1, replica_groups=mesh['gz'=32,'gy'=4] {'gz'}, dimensions={0} | all-to-all | bytes 196608 | tf_op jit(solution)/shard_map/while/body/eval_jaxpr/all_to_all | solution.py:139
  434.9 12.1 all_to_all.27
  466.6 6.9 collective-permute-start.7
  489.9 3.2 collective-permute-done.1
  495.3 4.7 collective-permute-start.3
  517.3 26.4 %all_to_all.26 = f32[32,2,384]{2,1,0:T(2,128)S(1)} all-to-all(f32[32,2,384]{2,1,0:T(2,128)S(1)} %reshape.356), channel_id=1, replica_groups=mesh['gz'=32,'gy'=4] {'gz'}, dimensions={0} | all-to-all | bytes 196608 | tf_op jit(solution)/shard_map/while/body/eval_jaxpr/all_to_all | solution.py:139
  545.2 12.1 all_to_all.27
  577.0 6.9 collective-permute-start.7
  600.3 3.2 collective-permute-done.1
  605.6 4.7 collective-permute-start.3
  627.7 26.4 %all_to_all.26 = f32[32,2,384]{2,1,0:T(2,128)S(1)} all-to-all(f32[32,2,384]{2,1,0:T(2,128)S(1)} %reshape.356), channel_id=1, replica_groups=mesh['gz'=32,'gy'=4] {'gz'}, dimensions={0} | all-to-all | bytes 196608 | tf_op jit(solution)/shard_map/while/body/eval_jaxpr/all_to_all | solution.py:139
  655.6 12.1 all_to_all.27
  687.4 6.9 collective-permute-start.7
  710.7 3.2 collective-permute-done.1
  716.0 4.7 collective-permute-start.3
  738.1 26.4 %all_to_all.26 = f32[32,2,384]{2,1,0:T(2,128)S(1)} all-to-all(f32[32,2,384]{2,1,0:T(2,128)S(1)} %reshape.356), channel_id=1, replica_groups=mesh['gz'=32,'gy'=4] {'gz'}, dimensions={0} | all-to-all | bytes 196608 | tf_op jit(solution)/shard_map/while/body/eval_jaxpr/all_to_all | solution.py:139
  766.0 12.1 all_to_all.27
  797.7 6.9 collective-permute-start.7
  821.0 3.2 collective-permute-done.1
  826.4 4.7 collective-permute-start.3
  848.4 26.4 %all_to_all.26 = f32[32,2,384]{2,1,0:T(2,128)S(1)} all-to-all(f32[32,2,384]{2,1,0:T(2,128)S(1)} %reshape.356), channel_id=1, replica_groups=mesh['gz'=32,'gy'=4] {'gz'}, dimensions={0} | all-to-all | bytes 196608 | tf_op jit(solution)/shard_map/while/body/eval_jaxpr/all_to_all | solution.py:139
  876.4 12.1 all_to_all.27
  908.1 6.9 collective-permute-start.7
  931.4 3.2 collective-permute-done.1
  936.7 4.7 collective-permute-start.3
  958.8 26.4 %all_to_all.26 = f32[32,2,384]{2,1,0:T(2,128)S(1)} all-to-all(f32[32,2,384]{2,1,0:T(2,128)S(1)} %reshape.356), channel_id=1, replica_groups=mesh['gz'=32,'gy'=4] {'gz'}, dimensions={0} | all-to-all | bytes 196608 | tf_op jit(solution)/shard_map/while/body/eval_jaxpr/all_to_all | solution.py:139
  986.7 12.1 all_to_all.27
  1018.5 6.9 collective-permute-start.7
  1047.1 4.7 collective-permute-start.3
  1069.2 26.4 %all_to_all.26 = f32[32,2,384]{2,1,0:T(2,128)S(1)} all-to-all(f32[32,2,384]{2,1,0:T(2,128)S(1)} %reshape.356), channel_id=1, replica_groups=mesh['gz'=32,'gy'=4] {'gz'}, dimensions={0} | all-to-all | bytes 196608 | tf_op jit(solution)/shard_map/while/body/eval_jaxpr/all_to_all | solution.py:139
  1097.1 12.1 all_to_all.27
  1128.8 6.9 collective-permute-start.7
  1157.5 4.7 collective-permute-start.3
  1179.5 26.4 %all_to_all.26 = f32[32,2,384]{2,1,0:T(2,128)S(1)} all-to-all(f32[32,2,384]{2,1,0:T(2,128)S(1)} %reshape.356), channel_id=1, replica_groups=mesh['gz'=32,'gy'=4] {'gz'}, dimensions={0} | all-to-all | bytes 196608 | tf_op jit(solution)/shard_map/while/body/eval_jaxpr/all_to_all | solution.py:139
  1207.5 12.1 all_to_all.27
  1239.2 6.9 collective-permute-start.7
  1267.9 4.7 collective-permute-start.3
  1289.9 26.4 %all_to_all.26 = f32[32,2,384]{2,1,0:T(2,128)S(1)} all-to-all(f32[32,2,384]{2,1,0:T(2,128)S(1)} %reshape.356), channel_id=1, replica_groups=mesh['gz'=32,'gy'=4] {'gz'}, dimensions={0} | all-to-all | bytes 196608 | tf_op jit(solution)/shard_map/while/body/eval_jaxpr/all_to_all | solution.py:139
  1317.8 12.1 all_to_all.27
  1349.6 6.9 collective-permute-start.7
  (1089 shorter events, 697.5 us)
Async XLA Ops:
  26.8 19.9 %all-to-all-start.2 = ((s32[32,1,2]{2,1,0:T(1,128)}), s32[32,1,2]{2,1,0:T(1,128)S(1)}, u32[]{:S(2)}, u32[]{:S(2)}) async-start(s32[32,1,2]{2,1,0:T(1,128)} %bitcast.27), calls=%async_computation.2 | async-start | bytes 32768 | tf_op jit(solution)/shard_map/all_to_all | solution.py:130
  50.3 6.4 collective-permute-start.1
  56.9 9.6 collective-permute-start.2
  132.1 14.0 %collective-permute-start.6 = (f32[3,20,2,256]{3,2,1,0:T(2,128)}, f32[3,20,2,256]{3,2,1,0:T(2,128)}, u32[]{:S(2)}, u32[]{:S(2)}) collective-permute-start(f32[3,20,2,256]{3,2,1,0:T(2,128)} %get-tuple-element.422), channel_id=1, source_target_pairs={{1,0},{2,1},{3,2},{5,4},{6,5},{7,6},{9,8},{10,9},{11,10},{13,12},{... | collective-permute-start | bytes 368648 | tf_op jit(solution)/shard_map/while/body/eval_jaxpr/ppermute | solution.py:24
  136.9 9.2 collective-permute-start.7
  155.6 6.5 collective-permute-start.1
  162.3 8.5 collective-permute-start.2
  164.3 7.8 collective-permute-start.3
  234.5 6.4 collective-permute-start.5
  243.3 12.9 collective-permute-start.6
  245.9 10.3 collective-permute-start.7
  272.6 8.6 collective-permute-start.2
  274.5 7.8 collective-permute-start.3
  344.9 6.4 collective-permute-start.5
  353.7 12.9 collective-permute-start.6
  356.3 10.3 collective-permute-start.7
  383.0 8.6 collective-permute-start.2
  384.9 7.8 collective-permute-start.3
  455.2 6.4 collective-permute-start.5
  464.0 12.9 collective-permute-start.6
  466.6 10.3 collective-permute-start.7
  493.3 8.6 collective-permute-start.2
  495.3 7.8 collective-permute-start.3
  565.6 6.4 collective-permute-start.5
  574.4 12.9 collective-permute-start.6
  577.0 10.3 collective-permute-start.7
  597.1 6.4 collective-permute-start.1
  603.7 8.6 collective-permute-start.2
  605.6 7.8 collective-permute-start.3
  676.0 6.4 collective-permute-start.5
  684.8 12.9 collective-permute-start.6
  687.4 10.3 collective-permute-start.7
  707.4 6.4 collective-permute-start.1
  714.1 8.6 collective-permute-start.2
  716.0 7.8 collective-permute-start.3
  786.4 6.4 collective-permute-start.5
  795.2 12.9 collective-permute-start.6
  797.7 10.3 collective-permute-start.7
  817.8 6.4 collective-permute-start.1
  824.4 8.6 collective-permute-start.2
  826.4 7.8 collective-permute-start.3
  896.7 6.4 collective-permute-start.5
  905.5 12.9 collective-permute-start.6
  908.1 10.3 collective-permute-start.7
  934.8 8.6 collective-permute-start.2
  936.7 7.8 collective-permute-start.3
  1007.1 6.4 collective-permute-start.5
  1015.9 12.9 collective-permute-start.6
  1018.5 10.3 collective-permute-start.7
  1045.2 8.6 collective-permute-start.2
  1047.1 7.8 collective-permute-start.3
  1117.5 6.4 collective-permute-start.5
  1126.3 12.9 collective-permute-start.6
  1128.8 10.3 collective-permute-start.7
  1155.6 8.6 collective-permute-start.2
  1157.5 7.8 collective-permute-start.3
  1227.8 6.4 collective-permute-start.5
  1236.6 12.9 collective-permute-start.6
  1239.2 10.3 collective-permute-start.7
  1265.9 8.6 collective-permute-start.2
  1267.9 7.8 collective-permute-start.3
  1338.2 6.4 collective-permute-start.5
  1347.0 12.9 collective-permute-start.6
  1349.6 10.3 collective-permute-start.7
  (167 other events, 735.8 us)
where the time goes:
time: 1380 us; the launch traced here: 1370 us
  blocking collectives  456 us (33%)
  starting transfers between devices  295 us (21%)
  other arithmetic  260 us (19%)
  local copies, waits for them, and re-layouts  232 us (17%)
  waiting for transfers between devices  108 us (8%)
    all_to_all x12, blocking collectives, couple(): lax.all_to_all(outgoing, 'gz', split_axis=0, concat_axis=0, tiled=True)  311 us
    ppermute x48, starting transfers between devices, with_halo(): before = lax.ppermute(last, axis, up)  194 us
    all_to_all x12, blocking collectives, couple(): lax.all_to_all(replies, 'gz', split_axis=0, concat_axis=0, tiled=True)  145 us
    ppermute x48, starting transfers between devices, with_halo(): after = lax.ppermute(initial, axis, down)  90.6 us
    ppermute x48, waiting for transfers between devices, with_halo(): after = lax.ppermute(initial, axis, down)  63.8 us
    another operation x36, local copies, waits for them, and re-layouts, velocity_update(): jnp.stack([vel[0] + time_step * buoy * force_x, vel[1] + time_step * buoy...  60.5 us
    while x60, other arithmetic  37.3 us
    ppermute x48, waiting for transfers between devices, with_halo(): before = lax.ppermute(last, axis, up)  37 us
  transfers between devices with their start and end apart: 97, of which 73 were waited for; matrix products, arithmetic and copies ran while one was open for 7% of the time, Pallas kernels for 0%

commit v1 on v0

v1 whole, which is shorter than its diff:
```python
import jax
import jax.numpy as jnp
from jax import lax
from jax.sharding import PartitionSpec as P
from jax.experimental import pallas as pl
from jax.experimental.pallas import tpu as pltpu

MESH = pl.DeviceIdType.MESH
STEPS = 12
CAP = 2
C1 = 9.0 / 8.0
C2 = -1.0 / 24.0
DT = 0.15
NGZ, NGY = 32, 4
CZ, CY, XB, LANE = 16, 16, 2, 128
POS = NGZ * CAP
YR, Y0 = 40, 10
VZ, V0 = CZ + 8, 4
SZ, S0 = CZ + 4, 2
F32 = jnp.float32
BF16 = jnp.bfloat16

OFFSETS = sorted(
    [(a, b, c) for a in range(2) for b in range(4) for c in range(4) if a + b + c > 0],
    key=lambda o: -(2 * o[0] + min(o[1], 4 - o[1]) + min(o[2], 4 - o[2])),
)


def xshift(f0, f1, by):
    lane = lax.broadcasted_iota(jnp.int32, f0.shape, 1)
    a = pltpu.roll(f0, (-by) % LANE, 1)
    b = pltpu.roll(f1, (-by) % LANE, 1)
    if by > 0:
        keep = lane < LANE - by
        return jnp.where(keep, a, b), jnp.where(keep, b, 0.0)
    keep = lane >= -by
    return jnp.where(keep, a, 0.0), jnp.where(keep, b, a)


def stencil(p, c, n, f, forward):
    return C1 * (n - c) + C2 * (f - p)


def dx(f0, f1, forward):
    up = xshift(f0, f1, 1)
    dn = xshift(f0, f1, -1)
    if forward:
        far = xshift(f0, f1, 2)
        return tuple(C1 * (up[i] - (f0, f1)[i]) + C2 * (far[i] - dn[i]) for i in range(2))
    far = xshift(f0, f1, -2)
    return tuple(C1 * ((f0, f1)[i] - dn[i]) + C2 * (up[i] - far[i]) for i in range(2))


def dmaj(load, forward):
    if forward:
        return C1 * (load(1) - load(0)) + C2 * (load(2) - load(-1))
    return C1 * (load(0) - load(-1)) + C2 * (load(1) - load(-2))


def kernel(
    state, region, lame, shear, buoyt, meta, bpos, gain,
    out, sens_out,
    V, S, own, dtb, sens, reg, bsend, brecv, csend, crecv, htab, onehot, rhs,
    mrecv, gtab, gs, srcv, srcs,
    lsem, bs, br, cs, cr, zs, zr, ys, yr, ms, mr, hs, hr,
):
    gz = lax.axis_index("gz")
    gy = lax.axis_index("gy")
    a0, b0, c0 = gz // 16, (gz // 4) % 4, gz % 4
    partners = [
        ((a0 + a) % 2) * 16 + ((b0 + b) % 4) * 4 + (c0 + c) % 4 for a, b, c in OFFSETS
    ]
    down, up = (gz + NGZ - 1) % NGZ, (gz + 1) % NGZ
    left, right = (gy + NGY - 1) % NGY, (gy + 1) % NGY
    has = {"down": gz > 0, "up": gz < NGZ - 1, "left": gy > 0, "right": gy < NGY - 1}

    zero = jnp.zeros((8, LANE), F32)

    def clear_v(l, c):
        for par in range(2):
            for f in range(3):
                for xb in range(XB):
                    for t in range(YR // 8):
                        V[par, f, l, xb, pl.ds(8 * t, 8), :] = zero
        return c

    lax.fori_loop(0, VZ, clear_v, 0)

    def clear_s(l, c):
        for f in range(8):
            for xb in range(XB):
                for t in range(YR // 8):
                    S[f, l, xb, pl.ds(8 * t, 8), :] = zero
        return c

    lax.fori_loop(0, SZ, clear_s, 0)

    def clear_c(l, c):
        csend[l] = zero
        return c

    lax.fori_loop(0, POS + 4, clear_c, 0)
    htab[32] = zero
    for f in range(3):
        rhs[f, 192:256, :] = jnp.zeros((64, 384), BF16)

    loads = []
    for xb in range(XB):
        cols = pl.ds(xb * LANE, LANE)
        loads.append(pltpu.make_async_copy(region.at[:, :, cols], reg.at[:, xb], lsem.at[0, xb]))
        loads.append(
            pltpu.make_async_copy(
                state.at[0:3, :, :, cols], V.at[0, :, V0 : V0 + CZ, xb, Y0 : Y0 + CY, :], lsem.at[1, xb]
            )
        )
        loads.append(
            pltpu.make_async_copy(
                state.at[3:9, :, :, cols], S.at[0:6, S0 : S0 + CZ, xb, Y0 : Y0 + CY, :], lsem.at[2, xb]
            )
        )
    for cp in loads:
        cp.start()

    barrier = pltpu.get_barrier_semaphore()
    for t in partners:
        pl.semaphore_signal(barrier, inc=1, device_id=(t, gy), device_id_type=MESH)
    for t in range(1, NGY):
        pl.semaphore_signal(barrier, inc=1, device_id=(gz, (gy + t) % NGY), device_id_type=MESH)

    for cp in loads:
        cp.wait()

    def material(l, c):
        for xb in range(XB):
            r = reg[l, xb]
            la = jnp.zeros((CY, LANE), F32)
            mu = jnp.zeros((CY, LANE), F32)
            bu = jnp.zeros((CY, LANE), F32)
            for v in range(8):
                hit = r == v
                la = jnp.where(hit, DT * lame[v], la)
                mu = jnp.where(hit, DT * shear[v], mu)
                bu = jnp.where(hit, DT * buoyt[v], bu)
            S[6, S0 + l, xb, pl.ds(Y0, CY), :] = la
            S[7, S0 + l, xb, pl.ds(Y0, CY), :] = mu
            dtb[l, xb] = bu
            for f in range(3):
                sens[f, l, xb] = jnp.zeros((CY, LANE), F32)
        return c

    lax.fori_loop(0, CZ, material, 0)
    pl.semaphore_wait(barrier, NGZ - 1 + NGY - 1)

    def remote(src, dst, s, r, to):
        return pltpu.make_async_remote_copy(
            src, dst, send_sem=s, recv_sem=r, device_id=to, device_id_type=MESH
        )

    def meta_copy(t):
        return remote(meta.at[0:2], mrecv.at[gz, 0:2], ms, mr, (t, gy))

    for t in partners:
        meta_copy(t).start()
    mrecv[gz] = meta[...]

    first = {
        "down": remote(S.at[3:8, 2:4, :, 10:26], S.at[3:8, 18:20, :, 10:26], hs.at[0], hr.at[0], (down, gy)),
        "up": remote(S.at[3:8, 16:18, :, 10:26], S.at[3:8, 0:2, :, 10:26], hs.at[1], hr.at[1], (up, gy)),
        "left": remote(S.at[1:4, 2:18, :, 10:12], S.at[1:4, 2:18, :, 26:28], hs.at[2], hr.at[2], (gz, left)),
        "right": remote(S.at[1:4, 2:18, :, 24:26], S.at[1:4, 2:18, :, 8:10], hs.at[3], hr.at[3], (gz, right)),
        "left2": remote(S.at[6:8, 2:18, :, 10:12], S.at[6:8, 2:18, :, 26:28], hs.at[4], hr.at[4], (gz, left)),
        "right2": remote(S.at[6:8, 2:18, :, 24:26], S.at[6:8, 2:18, :, 8:10], hs.at[5], hr.at[5], (gz, right)),
    }
    opposite = {"down": "up", "up": "down", "left": "right", "right": "left"}

    def start(copies):
        for name, cp in copies.items():
            pl.when(has[name.rstrip("2")])(cp.start)

    def wait_send(copies):
        for name, cp in copies.items():
            pl.when(has[name.rstrip("2")])(cp.wait_send)

    def wait_recv(copies):
        for name, cp in copies.items():
            pl.when(has[opposite[name.rstrip("2")]])(cp.wait_recv)

    start(first)

    all31 = mrecv.at[0 : NGZ - 1, 0:2]
    pltpu.make_async_copy(all31, all31, ms).wait()
    pltpu.make_async_copy(all31, all31, mr).wait()

    lane = lax.broadcasted_iota(jnp.int32, (NGZ, LANE), 1)
    dev = lax.broadcasted_iota(jnp.int32, (NGZ, LANE), 0)
    got = mrecv[:, 1, :]
    gtab[...] = got
    mine = (lane >= 2 * gz) & (lane < 2 * gz + 2)
    got = jnp.where(mine, got, -1)
    place = 2 * dev + lane - 2 * gz
    lane1 = lax.broadcasted_iota(jnp.int32, (8, LANE), 1)
    acc = jnp.zeros((8, LANE), jnp.int32)
    for s in range(32):
        total = jnp.sum(jnp.where(got == s, place, 0))
        acc = jnp.where(lane1 == s, total, acc)
    srcv[...] = jnp.minimum(acc, POS - 1)
    c1 = pltpu.make_async_copy(gtab, gs, lsem.at[0, 0])
    c2 = pltpu.make_async_copy(srcv, srcs, lsem.at[0, 1])
    c1.start()
    c2.start()

    row = lax.broadcasted_iota(jnp.int32, (CY, LANE), 0)
    lane16 = lax.broadcasted_iota(jnp.int32, (CY, LANE), 1)

    def ones(l, c):
        z = jnp.where(l < 3, l + 13, jnp.where(l < 19, l - 3, l - 19))
        who = jnp.where(l < 3, gz - 1, jnp.where(l < 19, gz, gz + 1))
        real = (who >= 0) & (who < NGZ)
        blk = mrecv[jnp.clip(who, 0, NGZ - 1), 0:1, :]
        blk = jnp.where(real, blk, -1)
        for xb in range(XB):
            hit = blk == z * 32 + row * 2 + xb
            start_row = pl.multiple_of(l * 32 + xb * 16, 16)
            onehot[pl.ds(start_row, 16), 0:128] = jnp.where(hit, 1.0, 0.0).astype(BF16)
            onehot[pl.ds(start_row, 16), 128:256] = jnp.where(hit & (lane16 < 64), 1.0, 0.0).astype(BF16)
        return c

    lax.fori_loop(0, CZ + 6, ones, 0)
    c1.wait()
    c2.wait()
    wait_send(first)
    wait_recv(first)

    def step(n, carry):
        p = lax.rem(n, 2)
        q = 1 - p

        def velocity(k, c):
            ks = k + S0
            for t in range(2):
                r0 = Y0 + 8 * t

                def s(f, xb, dz=0, dy=0):
                    return S[f, ks + dz, xb, pl.ds(r0 + dy, 8), :]

                xx = dx(s(0, 0), s(0, 1), True)
                xy = dx(s(2, 0), s(2, 1), False)
                xz = dx(s(5, 0), s(5, 1), False)
                for xb in range(XB):
                    fx = xx[xb] + dmaj(lambda o: s(2, xb, dy=o), False) + dmaj(lambda o: s(5, xb, dz=o), False)
                    fy = xy[xb] + dmaj(lambda o: s(1, xb, dy=o), True) + dmaj(lambda o: s(3, xb, dz=o), False)
                    fz = xz[xb] + dmaj(lambda o: s(3, xb, dy=o), False) + dmaj(lambda o: s(4, xb, dz=o), True)
                    bu = dtb[k, xb, pl.ds(8 * t, 8), :]
                    for f, force in enumerate((fx, fy, fz)):
                        new = V[p, f, k + V0, xb, pl.ds(r0, 8), :] + bu * force
                        V[q, f, k + V0, xb, pl.ds(r0, 8), :] = new
                        own[f, k, xb, pl.ds(8 * t, 8), :] = new
            return c

        lax.fori_loop(0, CZ, velocity, 0)

        def pick(i, c):
            for u in range(4):
                e = i * 4 + u
                b = bpos[0, 0, e]
                z, y, xb = b // 32, (b // 2) % 16, b % 2
                for f in range(3):
                    bsend[e, pl.ds(f, 1), :] = own[f, z, xb, pl.ds(y, 1), :]
            return c

        lax.fori_loop(0, POS // 4, pick, 0)

        def b_copy(t):
            return remote(
                bsend.at[pl.ds(2 * t, 2), 0:3], brecv.at[pl.ds(2 * gz, 2), 0:3], bs, br, (t, gy)
            )

        for t in partners:
            b_copy(t).start()
        for u in range(2):
            brecv[2 * gz + u] = bsend[2 * gz + u]

        zc = {
            "down": remote(V.at[q, :, 4:7, :, 10:26], V.at[q, :, 20:23, :, 10:26], zs.at[0], zr.at[q, 0], (down, gy)),
            "up": remote(V.at[q, :, 17:20, :, 10:26], V.at[q, :, 1:4, :, 10:26], zs.at[1], zr.at[q, 1], (up, gy)),
        }
        start(zc)

        ball = brecv.at[0 : POS - 2, 0:3]
        pltpu.make_async_copy(ball, ball, br).wait()

        for j in range(16):
            side0 = brecv[srcs[0, 2 * j]]
            side1 = brecv[srcs[0, 2 * j + 1]]
            slip = side0 - side1
            traction = gain[0, 0, j] * slip / jnp.sqrt(1.0 + slip * slip)
            htab[2 * j] = -0.5 * traction
            htab[2 * j + 1] = 0.5 * traction

        def reply(d, c):
            for u in range(2):
                slot = gs[d, 2 * gz + u]
                slot = jnp.where((slot < 0) | (slot > 32), 32, slot)
                csend[2 * d + 2 + u] = htab[slot]
            return c

        lax.fori_loop(0, NGZ, reply, 0)

        def c_copy(t):
            return remote(csend.at[pl.ds(2 * t, 6), 0:3], crecv.at[gz, :, 0:3], cs, cr, (t, gy))

        for t in partners:
            c_copy(t).start()
        for u in range(6):
            crecv[gz, u] = csend[2 * gz + u]

        pltpu.make_async_copy(ball, ball, bs).wait()
        wait_send(zc)
        wait_recv(zc)
        call = crecv.at[0 : NGZ - 1, :, 0:3]
        pltpu.make_async_copy(call, call, cr).wait()

        for g in range(3):
            for f in range(3):
                col = pl.ds(f * LANE, LANE)
                d = crecv[:, 2 * g : 2 * g + 2, f, :].reshape(POS, LANE)
                hi = d.astype(BF16)
                d = d - hi.astype(F32)
                mid = d.astype(BF16)
                lo = (d - mid.astype(F32)).astype(BF16)
                rhs[g, 0:64, col] = hi
                rhs[g, 64:128, col] = mid
                rhs[g, 128:192, col] = lo

        def apply(first_layer, layers, g):
            start_row = first_layer * 32
            if not isinstance(start_row, int):
                start_row = pl.multiple_of(start_row, 32)
            delta = jnp.dot(
                onehot[pl.ds(start_row, layers * 32), :], rhs[g], preferred_element_type=F32
            )
            for l in range(layers):
                for xb in range(XB):
                    for f in range(3):
                        r = l * 32 + xb * 16
                        here = V[q, f, first_layer + 1 + l, xb, pl.ds(Y0, CY), :]
                        V[q, f, first_layer + 1 + l, xb, pl.ds(Y0, CY), :] = (
                            here + delta[r : r + 16, f * LANE : (f + 1) * LANE]
                        )

        apply(0, 3, 0)
        apply(19, 3, 2)

        def apply_own(i, c):
            apply(3 + 4 * i, 4, 1)
            return c

        lax.fori_loop(0, 4, apply_own, 0)
        pltpu.make_async_copy(call, call, cs).wait()

        yc = {
            "left": remote(V.at[q, :, 1:23, :, 10:13], V.at[q, :, 1:23, :, 26:29], ys.at[0], yr.at[q, 0], (gz, left)),
            "right": remote(V.at[q, :, 1:23, :, 23:26], V.at[q, :, 1:23, :, 7:10], ys.at[1], yr.at[q, 1], (gz, right)),
        }
        start(yc)

        def sensitivity(k, c):
            for f in range(3):
                for xb in range(XB):
                    sens[f, k, xb] = sens[f, k, xb] + DT * V[q, f, k + V0, xb, pl.ds(Y0, CY), :]
            return c

        lax.fori_loop(0, CZ, sensitivity, 0)
        wait_send(yc)
        wait_recv(yc)

        def stress(k, c):
            kv = k + 2
            for t in range(3):
                r0 = 8 + 8 * t

                def v(f, xb, dz=0, dy=0):
                    return V[q, f, kv + dz, xb, pl.ds(r0 + dy, 8), :]

                exs = dx(v(0, 0), v(0, 1), False)
                vyx = dx(v(1, 0), v(1, 1), True)
                vzx = dx(v(2, 0), v(2, 1), True)
                for xb in range(XB):
                    ex = exs[xb]
                    ey = dmaj(lambda o: v(1, xb, dy=o), False)
                    ez = dmaj(lambda o: v(2, xb, dz=o), False)
                    la = S[6, k, xb, pl.ds(r0, 8), :]
                    mu = S[7, k, xb, pl.ds(r0, 8), :]
                    mu2 = mu + mu
                    div = la * (ex + ey + ez)
                    new = (
                        div + mu2 * ex,
                        div + mu2 * ey,
                        mu * (dmaj(lambda o: v(0, xb, dy=o), True) + vyx[xb]),
                        mu * (dmaj(lambda o: v(1, xb, dz=o), True) + dmaj(lambda o: v(2, xb, dy=o), True)),
                        div + mu2 * ez,
                        mu * (dmaj(lambda o: v(0, xb, dz=o), True) + vzx[xb]),
                    )
                    for f in range(6):
                        S[f, k, xb, pl.ds(r0, 8), :] = S[f, k, xb, pl.ds(r0, 8), :] + new[f]
            return c

        lax.fori_loop(0, SZ, stress, 0)
        return carry

    lax.fori_loop(0, STEPS, step, 0)

    last = STEPS % 2
    stores = []
    for xb in range(XB):
        cols = pl.ds(xb * LANE, LANE)
        stores.append(
            pltpu.make_async_copy(
                V.at[last, :, V0 : V0 + CZ, xb, Y0 : Y0 + CY, :], out.at[0:3, :, :, cols], lsem.at[0, xb]
            )
        )
        stores.append(
            pltpu.make_async_copy(
                S.at[0:6, S0 : S0 + CZ, xb, Y0 : Y0 + CY, :], out.at[3:9, :, :, cols], lsem.at[1, xb]
            )
        )
        stores.append(pltpu.make_async_copy(sens.at[:, :, xb], sens_out.at[:, :, :, cols], lsem.at[2, xb]))
    for cp in stores:
        cp.start()
    for cp in stores:
        cp.wait()


def per_device(state, region, lame, shear, buoyt, face_block, face_owner, face_slot, joint_gain):
    blocks, owners, slots = face_block.reshape(-1), face_owner.reshape(-1), face_slot.reshape(-1)
    ids = jnp.arange(blocks.shape[0], dtype=jnp.int32)
    earlier = (owners[None, :] == owners[:, None]) & (ids[None, :] < ids[:, None])
    position = owners * CAP + jnp.sum(earlier.astype(jnp.int32), axis=1)
    match = jnp.arange(POS, dtype=jnp.int32)[:, None] == position[None, :]
    block_at = jnp.sum(jnp.where(match, blocks[None, :] + 1, 0), axis=1) - 1
    slot_at = jnp.sum(jnp.where(match, slots[None, :] + 1, 0), axis=1) - 1
    meta = jnp.concatenate([block_at, block_at, slot_at, slot_at]).reshape(2, LANE)
    meta = jnp.concatenate([meta, jnp.zeros((6, LANE), jnp.int32)], axis=0)
    bpos = jnp.maximum(block_at, 0).reshape(1, 1, POS)
    smem = pl.BlockSpec(memory_space=pltpu.SMEM)
    vmem = pl.BlockSpec(memory_space=pltpu.VMEM)
    anym = pl.BlockSpec(memory_space=pl.ANY)
    dma = pltpu.SemaphoreType.DMA
    return pl.pallas_call(
        kernel,
        out_shape=(
            jax.ShapeDtypeStruct(state.shape, F32),
            jax.ShapeDtypeStruct((3,) + state.shape[1:], F32),
        ),
        in_specs=[anym, anym, smem, smem, smem, vmem, smem, smem],
        out_specs=(anym, anym),
        scratch_shapes=[
            pltpu.VMEM((2, 3, VZ, XB, YR, LANE), F32),
            pltpu.VMEM((8, SZ, XB, YR, LANE), F32),
            pltpu.VMEM((3, CZ, XB, CY, LANE), F32),
            pltpu.VMEM((CZ, XB, CY, LANE), F32),
            pltpu.VMEM((3, CZ, XB, CY, LANE), F32),
            pltpu.VMEM((CZ, XB, CY, LANE), jnp.int32),
            pltpu.VMEM((POS, 8, LANE), F32),
            pltpu.VMEM((POS, 8, LANE), F32),
            pltpu.VMEM((POS + 4, 8, LANE), F32),
            pltpu.VMEM((NGZ, 6, 8, LANE), F32),
            pltpu.VMEM((33, 8, LANE), F32),
            pltpu.VMEM(((CZ + 6) * 32, 256), BF16),
            pltpu.VMEM((3, 256, 3 * LANE), BF16),
            pltpu.VMEM((NGZ, 8, LANE), jnp.int32),
            pltpu.VMEM((NGZ, LANE), jnp.int32),
            pltpu.SMEM((NGZ, LANE), jnp.int32),
            pltpu.VMEM((8, LANE), jnp.int32),
            pltpu.SMEM((8, LANE), jnp.int32),
            dma((3, 2)),
            dma,
            dma,
            dma,
            dma,
            dma((2,)),
            dma((2, 2)),
            dma((2,)),
            dma((2, 2)),
            dma,
            dma,
            dma((6,)),
            dma((6,)),
        ],
        compiler_params=pltpu.CompilerParams(
            collective_id=0, has_side_effects=True, vmem_limit_bytes=40 * 1024 * 1024
        ),
    )(state, region, lame, shear, buoyt, meta, bpos, joint_gain)


def solution(mesh):
    grid = P("gz", "gy", None)
    field = P(None, "gz", "gy", None)
    return jax.shard_map(
        per_device,
        mesh=mesh,
        in_specs=(field, grid, P(), P(), P(), grid, grid, grid, grid),
        out_specs=(field, field),
        check_vma=False,
    )
```

time: 1380 us -> 316 us (0.23)
  blocking collectives: 456 us -> 0 us
  Pallas kernels: 0 us -> 304 us
  starting transfers between devices: 295 us -> 0 us
  other arithmetic: 260 us -> 3.07 us
  local copies, waits for them, and re-layouts: 232 us -> 7.53 us
  waiting for transfers between devices: 108 us -> 0 us
    all_to_all x24 -> x0, blocking collectives: 456 us -> none  [the longest x12 311 us: couple(): lax.all_to_all(outgoing, 'gz', split_axis=0, concat_axis=0, tiled=True)]
    pallas_call x0 -> x1, Pallas kernels: none -> 304 us  [per_device(): pl.pallas_call(kernel, out_shape=(jax.ShapeDtypeStruct(state.shape, F32),...]
    ppermute x96 -> x0, starting transfers between devices: 284 us -> none  [the longest x48 194 us: with_halo(): before = lax.ppermute(last, axis, up)]
    add x53 -> x3, other arithmetic: 129 us -> 1.98 us  [the longest x1 0.66 us: per_device(): position = owners * CAP + jnp.sum(earlier.astype(jnp.int32), axis=1)]
    ppermute x96 -> x0, waiting for transfers between devices: 101 us -> none  [the longest x48 63.8 us: with_halo(): after = lax.ppermute(initial, axis, down)]
    another operation x48 -> x0, local copies, waits for them, and re-layouts: 60.9 us -> none  [the longest x36 60.5 us: velocity_update(): jnp.stack([vel[0] + time_step * buoy * force_x, vel[1] + time_step * buoy...]
    slice x90 -> x0, local copies, waits for them, and re-layouts: 55.7 us -> none  [the longest x12 24.7 us: stress_update(): vel[1]]
    while x60 -> x0, other arithmetic: 37.3 us -> none
  transfers between devices with their start and end apart: 97 -> 0, of which waited for: 73 -> 0; matrix products, arithmetic and copies ran while one was open for 7% -> 0% of each run, Pallas kernels for 0% -> 0%
where the time goes in v1:
time: 316 us
  Pallas kernels  304 us (96%)
  local copies, waits for them, and re-layouts  7.53 us (2%)
    pallas_call x1, Pallas kernels, per_device(): pl.pallas_call(kernel, out_shape=(jax.ShapeDtypeStruct(state.shape, F32),...  304 us
    unnamed x14, local copies, waits for them, and re-layouts  7.52 us

profile of v1, /device:TPU:1, one launch (start us, length us, event | category | flops | bytes accessed | tf_op | source)
XLA Modules:
  0.0 315.5 jit_solution(7807866902305538580)
XLA Ops:
  0.6 0.7 add_bitcast_fusion.2
  1.3 0.7 add_bitcast_fusion.1
  1.9 0.9 convert_reduce_fusion
  2.9 0.7 multiply_add_fusion
  3.5 0.1 select_reduce_fusion.1
  3.6 0.1 add_bitcast_fusion
  3.7 0.0 copy-start
  3.7 1.7 copy-done
  5.4 0.0 copy-start.1
  5.4 0.9 copy-done.1
  6.3 0.0 copy-start.2
  6.3 0.7 copy-done.2
  7.0 0.0 copy-start.3
  7.0 0.7 copy-done.3
  7.6 0.0 copy-start.4
  7.6 0.7 copy-done.4
  8.3 0.0 copy-start.5
  8.3 0.7 copy-done.5
  9.0 304.3 %shard_map.104 = (f32[9,16,16,256]{3,2,1,0:T(8,128)S(1)}, f32[3,16,16,256]{3,2,1,0:T(8,128)S(1)}) custom-call(f32[9,16,16,256]{3,2,1,0:T(8,128)S(1)} %copy-done, s32[16,16,256]{2,1,0:T(8,128)S(1)} %copy-done.1, f32[8]{0:T(128)S(1)} %copy-done.2, f32[8]{0:T(128)S(1)} %copy-done.3, f32[8]{0:T(128)S(1)} %copy-done.4, s32[8,128]{1,0:T(8,128)S(1)} %concatenate.7.meta, ...), custom_call_target="tpu_custom_call" | custom-call | tf_op jit(solution)/shard_map/pallas_call | solution.py:449
  313.2 1.4 copy.13
  314.6 0.9 copy.14
  (2 shorter events, 0.0 us)
Async XLA Ops:
  3.7 1.7 copy-start
  5.4 0.9 copy-start.1
  6.3 0.7 copy-start.2
  7.0 0.7 copy-start.3
  7.6 0.7 copy-start.4
  8.3 0.7 copy-start.5

commit v2 on v1

--- a/solution.py
+++ b/solution.py
@@ -1,3 +1,5 @@
+import functools
+
 import jax
 import jax.numpy as jnp
 from jax import lax
@@ -14,7 +16,7 @@
 NGZ, NGY = 32, 4
 CZ, CY, XB, LANE = 16, 16, 2, 128
 POS = NGZ * CAP
-YR, Y0 = 40, 10
+YR, Y0 = 40, 14
 VZ, V0 = CZ + 8, 4
 SZ, S0 = CZ + 4, 2
 F32 = jnp.float32
@@ -58,10 +60,10 @@
 
 
 def kernel(
-    state, region, lame, shear, buoyt, meta, bpos, gain,
+    state, region, lame, shear, buoyt, fblock, fowner, fslot, gain,
     out, sens_out,
     V, S, own, dtb, sens, reg, bsend, brecv, csend, crecv, htab, onehot, rhs,
-    mrecv, gtab, gs, srcv, srcs,
+    meta, mrecv, gtab, gs, srcv, srcs, bposv, bpos,
     lsem, bs, br, cs, cr, zs, zr, ys, yr, ms, mr, hs, hr,
 ):
     gz = lax.axis_index("gz")
@@ -73,36 +75,6 @@
     down, up = (gz + NGZ - 1) % NGZ, (gz + 1) % NGZ
     left, right = (gy + NGY - 1) % NGY, (gy + 1) % NGY
     has = {"down": gz > 0, "up": gz < NGZ - 1, "left": gy > 0, "right": gy < NGY - 1}
-
-    zero = jnp.zeros((8, LANE), F32)
-
-    def clear_v(l, c):
-        for par in range(2):
-            for f in range(3):
-                for xb in range(XB):
-                    for t in range(YR // 8):
-                        V[par, f, l, xb, pl.ds(8 * t, 8), :] = zero
-        return c
-
-    lax.fori_loop(0, VZ, clear_v, 0)
-
-    def clear_s(l, c):
-        for f in range(8):
-            for xb in range(XB):
-                for t in range(YR // 8):
-                    S[f, l, xb, pl.ds(8 * t, 8), :] = zero
-        return c
-
-    lax.fori_loop(0, SZ, clear_s, 0)
-
-    def clear_c(l, c):
-        csend[l] = zero
-        return c
-
-    lax.fori_loop(0, POS + 4, clear_c, 0)
-    htab[32] = zero
-    for f in range(3):
-        rhs[f, 192:256, :] = jnp.zeros((64, 384), BF16)
 
     loads = []
     for xb in range(XB):
@@ -120,6 +92,63 @@
         )
     for cp in loads:
         cp.start()
+
+    zero = jnp.zeros((8, LANE), F32)
+    zero16 = jnp.zeros((CY, LANE), F32)
+
+    def edges(ref, idx):
+        for xb in range(XB):
+            ref[(*idx, xb, pl.ds(Y0 - 8, 8), slice(None))] = zero
+            ref[(*idx, xb, pl.ds(Y0 + CY, 8), slice(None))] = zero
+
+    def clear_v(l, c):
+        for par in range(2):
+            for f in range(3):
+                edges(V, (par, f, l))
+        return c
+
+    lax.fori_loop(0, VZ, clear_v, 0)
+
+    def clear_s(l, c):
+        for f in range(8):
+            edges(S, (f, l))
+        return c
+
+    lax.fori_loop(0, SZ, clear_s, 0)
+
+    def clear_layers(l, c):
+        for xb in range(XB):
+            for base in (0, V0 + CZ):
+                for par in range(2):
+                    for f in range(3):
+                        V[par, f, base + l, xb, pl.ds(Y0, CY), :] = zero16
+        return c
+
+    lax.fori_loop(0, V0, clear_layers, 0)
+    for l in (0, 1, S0 + CZ, S0 + CZ + 1):
+        for xb in range(XB):
+            for f in range(8):
+                S[f, l, xb, pl.ds(Y0, CY), :] = zero16
+    for f in range(3):
+        csend[f, 0:8, :] = zero
+        csend[f, 64:72, :] = zero
+        rhs[f, 192:256, :] = jnp.zeros((64, 384), BF16)
+    htab[32] = zero
+
+    lane8 = lax.broadcasted_iota(jnp.int32, (8, LANE), 1)
+    lane_owner, lane_rank = lane8 % 32, (lane8 // 32) % 2
+    count = jnp.zeros((8, LANE), jnp.int32)
+    block_at = jnp.full((8, LANE), -1, jnp.int32)
+    slot_at = jnp.full((8, LANE), -1, jnp.int32)
+    for e in range(32):
+        to = lane_owner == fowner[0, 0, e]
+        here = to & (lane_rank == count)
+        block_at = jnp.where(here, fblock[0, 0, e], block_at)
+        slot_at = jnp.where(here, fslot[0, 0, e], slot_at)
+        count = jnp.where(to, count + 1, count)
+    sub = lax.broadcasted_iota(jnp.int32, (8, LANE), 0)
+    meta[...] = jnp.where(sub == 0, block_at, slot_at)
+    bposv[...] = jnp.clip(block_at, 0, 511)
 
     barrier = pltpu.get_barrier_semaphore()
     for t in partners:
@@ -164,12 +193,12 @@
     mrecv[gz] = meta[...]
 
     first = {
-        "down": remote(S.at[3:8, 2:4, :, 10:26], S.at[3:8, 18:20, :, 10:26], hs.at[0], hr.at[0], (down, gy)),
-        "up": remote(S.at[3:8, 16:18, :, 10:26], S.at[3:8, 0:2, :, 10:26], hs.at[1], hr.at[1], (up, gy)),
-        "left": remote(S.at[1:4, 2:18, :, 10:12], S.at[1:4, 2:18, :, 26:28], hs.at[2], hr.at[2], (gz, left)),
-        "right": remote(S.at[1:4, 2:18, :, 24:26], S.at[1:4, 2:18, :, 8:10], hs.at[3], hr.at[3], (gz, right)),
-        "left2": remote(S.at[6:8, 2:18, :, 10:12], S.at[6:8, 2:18, :, 26:28], hs.at[4], hr.at[4], (gz, left)),
-        "right2": remote(S.at[6:8, 2:18, :, 24:26], S.at[6:8, 2:18, :, 8:10], hs.at[5], hr.at[5], (gz, right)),
+        "down": remote(S.at[3:8, 2:4, :, 14:30], S.at[3:8, 18:20, :, 14:30], hs.at[0], hr.at[0], (down, gy)),
+        "up": remote(S.at[3:8, 16:18, :, 14:30], S.at[3:8, 0:2, :, 14:30], hs.at[1], hr.at[1], (up, gy)),
+        "left": remote(S.at[1:4, 2:18, :, 14:16], S.at[1:4, 2:18, :, 30:32], hs.at[2], hr.at[2], (gz, left)),
+        "right": remote(S.at[1:4, 2:18, :, 28:30], S.at[1:4, 2:18, :, 12:14], hs.at[3], hr.at[3], (gz, right)),
+        "left2": remote(S.at[6:8, 2:18, :, 14:16], S.at[6:8, 2:18, :, 30:32], hs.at[4], hr.at[4], (gz, left)),
+        "right2": remote(S.at[6:8, 2:18, :, 28:30], S.at[6:8, 2:18, :, 12:14], hs.at[5], hr.at[5], (gz, right)),
     }
     opposite = {"down": "up", "up": "down", "left": "right", "right": "left"}
 
@@ -195,9 +224,9 @@
     dev = lax.broadcasted_iota(jnp.int32, (NGZ, LANE), 0)
     got = mrecv[:, 1, :]
     gtab[...] = got
-    mine = (lane >= 2 * gz) & (lane < 2 * gz + 2)
+    mine = (lane == gz) | (lane == gz + 32)
     got = jnp.where(mine, got, -1)
-    place = 2 * dev + lane - 2 * gz
+    place = 2 * dev + jnp.where(lane == gz + 32, 1, 0)
     lane1 = lax.broadcasted_iota(jnp.int32, (8, LANE), 1)
     acc = jnp.zeros((8, LANE), jnp.int32)
     for s in range(32):
@@ -206,8 +235,10 @@
     srcv[...] = jnp.minimum(acc, POS - 1)
     c1 = pltpu.make_async_copy(gtab, gs, lsem.at[0, 0])
     c2 = pltpu.make_async_copy(srcv, srcs, lsem.at[0, 1])
+    c3 = pltpu.make_async_copy(bposv, bpos, lsem.at[1, 0])
     c1.start()
     c2.start()
+    c3.start()
 
     row = lax.broadcasted_iota(jnp.int32, (CY, LANE), 0)
     lane16 = lax.broadcasted_iota(jnp.int32, (CY, LANE), 1)
@@ -228,6 +259,7 @@
     lax.fori_loop(0, CZ + 6, ones, 0)
     c1.wait()
     c2.wait()
+    c3.wait()
     wait_send(first)
     wait_recv(first)
 
@@ -253,22 +285,20 @@
                     bu = dtb[k, xb, pl.ds(8 * t, 8), :]
                     for f, force in enumerate((fx, fy, fz)):
                         new = V[p, f, k + V0, xb, pl.ds(r0, 8), :] + bu * force
-                        V[q, f, k + V0, xb, pl.ds(r0, 8), :] = new
                         own[f, k, xb, pl.ds(8 * t, 8), :] = new
             return c
 
-        lax.fori_loop(0, CZ, velocity, 0)
-
-        def pick(i, c):
-            for u in range(4):
-                e = i * 4 + u
-                b = bpos[0, 0, e]
+        lax.fori_loop(0, CZ, velocity, 0, unroll=4)
+
+        def pick(d, c):
+            for u in range(2):
+                b = bpos[0, u * 32 + d]
                 z, y, xb = b // 32, (b // 2) % 16, b % 2
                 for f in range(3):
-                    bsend[e, pl.ds(f, 1), :] = own[f, z, xb, pl.ds(y, 1), :]
+                    bsend[2 * d + u, pl.ds(f, 1), :] = own[f, z, xb, pl.ds(y, 1), :]
             return c
 
-        lax.fori_loop(0, POS // 4, pick, 0)
+        lax.fori_loop(0, NGZ, pick, 0, unroll=8)
 
         def b_copy(t):
             return remote(
@@ -281,8 +311,8 @@
             brecv[2 * gz + u] = bsend[2 * gz + u]
 
         zc = {
-            "down": remote(V.at[q, :, 4:7, :, 10:26], V.at[q, :, 20:23, :, 10:26], zs.at[0], zr.at[q, 0], (down, gy)),
-            "up": remote(V.at[q, :, 17:20, :, 10:26], V.at[q, :, 1:4, :, 10:26], zs.at[1], zr.at[q, 1], (up, gy)),
+            "down": remote(own.at[:, 0:3], V.at[q, :, 20:23, :, 14:30], zs.at[0], zr.at[q, 0], (down, gy)),
+            "up": remote(own.at[:, 13:16], V.at[q, :, 1:4, :, 14:30], zs.at[1], zr.at[q, 1], (up, gy)),
         }
         start(zc)
 
@@ -299,31 +329,35 @@
 
         def reply(d, c):
             for u in range(2):
-                slot = gs[d, 2 * gz + u]
+                slot = gs[d, u * 32 + gz]
                 slot = jnp.where((slot < 0) | (slot > 32), 32, slot)
-                csend[2 * d + 2 + u] = htab[slot]
+                for f in range(3):
+                    csend[f, pl.ds(2 * d + 2 + u, 1), :] = htab[slot, pl.ds(f, 1), :]
             return c
 
-        lax.fori_loop(0, NGZ, reply, 0)
+        lax.fori_loop(0, NGZ, reply, 0, unroll=8)
 
         def c_copy(t):
-            return remote(csend.at[pl.ds(2 * t, 6), 0:3], crecv.at[gz, :, 0:3], cs, cr, (t, gy))
+            return remote(csend.at[:, pl.ds(2 * t, 6)], crecv.at[:, pl.ds(6 * gz, 6)], cs, cr, (t, gy))
 
         for t in partners:
             c_copy(t).start()
         for u in range(6):
-            crecv[gz, u] = csend[2 * gz + u]
+            for f in range(3):
+                crecv[f, pl.ds(6 * gz + u, 1), :] = csend[f, pl.ds(2 * gz + u, 1), :]
 
         pltpu.make_async_copy(ball, ball, bs).wait()
         wait_send(zc)
         wait_recv(zc)
-        call = crecv.at[0 : NGZ - 1, :, 0:3]
+        call = crecv.at[:, 0 : 6 * (NGZ - 1)]
         pltpu.make_async_copy(call, call, cr).wait()
 
         for g in range(3):
             for f in range(3):
                 col = pl.ds(f * LANE, LANE)
-                d = crecv[:, 2 * g : 2 * g + 2, f, :].reshape(POS, LANE)
+                d = jnp.concatenate(
+                    [crecv[f, pl.ds(2 * g + r, NGZ, stride=6), :] for r in range(2)], axis=0
+                )
                 hi = d.astype(BF16)
                 d = d - hi.astype(F32)
                 mid = d.astype(BF16)
@@ -333,34 +367,28 @@
                 rhs[g, 128:192, col] = lo
 
         def apply(first_layer, layers, g):
-            start_row = first_layer * 32
-            if not isinstance(start_row, int):
-                start_row = pl.multiple_of(start_row, 32)
             delta = jnp.dot(
-                onehot[pl.ds(start_row, layers * 32), :], rhs[g], preferred_element_type=F32
+                onehot[pl.ds(first_layer * 32, layers * 32), :], rhs[g], preferred_element_type=F32
             )
             for l in range(layers):
+                at = first_layer + 1 + l
                 for xb in range(XB):
                     for f in range(3):
                         r = l * 32 + xb * 16
-                        here = V[q, f, first_layer + 1 + l, xb, pl.ds(Y0, CY), :]
-                        V[q, f, first_layer + 1 + l, xb, pl.ds(Y0, CY), :] = (
+                        here = own[f, at - V0, xb] if g == 1 else V[q, f, at, xb, pl.ds(Y0, CY), :]
+                        V[q, f, at, xb, pl.ds(Y0, CY), :] = (
                             here + delta[r : r + 16, f * LANE : (f + 1) * LANE]
                         )
 
         apply(0, 3, 0)
         apply(19, 3, 2)
-
-        def apply_own(i, c):
-            apply(3 + 4 * i, 4, 1)
-            return c
-
-        lax.fori_loop(0, 4, apply_own, 0)
+        apply(3, 8, 1)
+        apply(11, 8, 1)
         pltpu.make_async_copy(call, call, cs).wait()
 
         yc = {
-            "left": remote(V.at[q, :, 1:23, :, 10:13], V.at[q, :, 1:23, :, 26:29], ys.at[0], yr.at[q, 0], (gz, left)),
-            "right": remote(V.at[q, :, 1:23, :, 23:26], V.at[q, :, 1:23, :, 7:10], ys.at[1], yr.at[q, 1], (gz, right)),
+            "left": remote(V.at[q, :, 1:23, :, 14:17], V.at[q, :, 1:23, :, 30:33], ys.at[0], yr.at[q, 0], (gz, left)),
+            "right": remote(V.at[q, :, 1:23, :, 27:30], V.at[q, :, 1:23, :, 11:14], ys.at[1], yr.at[q, 1], (gz, right)),
         }
         start(yc)
 
@@ -370,13 +398,11 @@
                     sens[f, k, xb] = sens[f, k, xb] + DT * V[q, f, k + V0, xb, pl.ds(Y0, CY), :]
             return c
 
-        lax.fori_loop(0, CZ, sensitivity, 0)
-        wait_send(yc)
-        wait_recv(yc)
-
-        def stress(k, c):
+        lax.fori_loop(0, CZ, sensitivity, 0, unroll=4)
+
+        def stress(tiles, k, c):
             kv = k + 2
-            for t in range(3):
+            for t in tiles:
                 r0 = 8 + 8 * t
 
                 def v(f, xb, dz=0, dy=0):
@@ -405,7 +431,10 @@
                         S[f, k, xb, pl.ds(r0, 8), :] = S[f, k, xb, pl.ds(r0, 8), :] + new[f]
             return c
 
-        lax.fori_loop(0, SZ, stress, 0)
+        lax.fori_loop(0, SZ, functools.partial(stress, (1,)), 0, unroll=5)
+        wait_send(yc)
+        wait_recv(yc)
+        lax.fori_loop(0, SZ, functools.partial(stress, (0, 2)), 0, unroll=4)
         return carry
 
     lax.fori_loop(0, STEPS, step, 0)
@@ -432,19 +461,9 @@
 
 
 def per_device(state, region, lame, shear, buoyt, face_block, face_owner, face_slot, joint_gain):
-    blocks, owners, slots = face_block.reshape(-1), face_owner.reshape(-1), face_slot.reshape(-1)
-    ids = jnp.arange(blocks.shape[0], dtype=jnp.int32)
-    earlier = (owners[None, :] == owners[:, None]) & (ids[None, :] < ids[:, None])
-    position = owners * CAP + jnp.sum(earlier.astype(jnp.int32), axis=1)
-    match = jnp.arange(POS, dtype=jnp.int32)[:, None] == position[None, :]
-    block_at = jnp.sum(jnp.where(match, blocks[None, :] + 1, 0), axis=1) - 1
-    slot_at = jnp.sum(jnp.where(match, slots[None, :] + 1, 0), axis=1) - 1
-    meta = jnp.concatenate([block_at, block_at, slot_at, slot_at]).reshape(2, LANE)
-    meta = jnp.concatenate([meta, jnp.zeros((6, LANE), jnp.int32)], axis=0)
-    bpos = jnp.maximum(block_at, 0).reshape(1, 1, POS)
     smem = pl.BlockSpec(memory_space=pltpu.SMEM)
-    vmem = pl.BlockSpec(memory_space=pltpu.VMEM)
     anym = pl.BlockSpec(memory_space=pl.ANY)
+    hbm = pl.BlockSpec(memory_space=pltpu.HBM)
     dma = pltpu.SemaphoreType.DMA
     return pl.pallas_call(
         kernel,
@@ -452,7 +471,7 @@
             jax.ShapeDtypeStruct(state.shape, F32),
             jax.ShapeDtypeStruct((3,) + state.shape[1:], F32),
         ),
-        in_specs=[anym, anym, smem, smem, smem, vmem, smem, smem],
+        in_specs=[hbm, hbm] + [smem] * 7,
         out_specs=(anym, anym),
         scratch_shapes=[
             pltpu.VMEM((2, 3, VZ, XB, YR, LANE), F32),
@@ -463,14 +482,17 @@
             pltpu.VMEM((CZ, XB, CY, LANE), jnp.int32),
             pltpu.VMEM((POS, 8, LANE), F32),
             pltpu.VMEM((POS, 8, LANE), F32),
-            pltpu.VMEM((POS + 4, 8, LANE), F32),
-            pltpu.VMEM((NGZ, 6, 8, LANE), F32),
+            pltpu.VMEM((3, POS + 8, LANE), F32),
+            pltpu.VMEM((3, 6 * NGZ, LANE), F32),
             pltpu.VMEM((33, 8, LANE), F32),
             pltpu.VMEM(((CZ + 6) * 32, 256), BF16),
             pltpu.VMEM((3, 256, 3 * LANE), BF16),
+            pltpu.VMEM((8, LANE), jnp.int32),
             pltpu.VMEM((NGZ, 8, LANE), jnp.int32),
             pltpu.VMEM((NGZ, LANE), jnp.int32),
             pltpu.SMEM((NGZ, LANE), jnp.int32),
+            pltpu.VMEM((8, LANE), jnp.int32),
+            pltpu.SMEM((8, LANE), jnp.int32),
             pltpu.VMEM((8, LANE), jnp.int32),
             pltpu.SMEM((8, LANE), jnp.int32),
             dma((3, 2)),
@@ -488,9 +510,9 @@
             dma((6,)),
         ],
         compiler_params=pltpu.CompilerParams(
-            collective_id=0, has_side_effects=True, vmem_limit_bytes=40 * 1024 * 1024
+            collective_id=0, has_side_effects=True, vmem_limit_bytes=60 * 1024 * 1024
         ),
-    )(state, region, lame, shear, buoyt, meta, bpos, joint_gain)
+    )(state, region, lame, shear, buoyt, face_block, face_owner, face_slot, joint_gain)
 
 
 def solution(mesh):

time: 316 us -> 254 us (0.80)
  Pallas kernels: 304 us -> 249 us
  local copies, waits for them, and re-layouts: 7.53 us -> 4.23 us
    pallas_call x1, Pallas kernels: 304 us -> 249 us  [per_device(): pl.pallas_call(kernel, out_shape=(jax.ShapeDtypeStruct(state.shape, F32),...]
    unnamed x14 -> x4, local copies, waits for them, and re-layouts: 7.52 us -> 4.23 us
where the time goes in v2:
time: 254 us
  Pallas kernels  249 us (98%)
  local copies, waits for them, and re-layouts  4.23 us (2%)
    pallas_call x1, Pallas kernels, per_device(): pl.pallas_call(kernel, out_shape=(jax.ShapeDtypeStruct(state.shape, F32),...  249 us

profile of v2, /device:TPU:1, one launch (start us, length us, event | category | flops | bytes accessed | tf_op | source)
XLA Modules:
  0.0 253.9 jit_solution(16194712559113013745)
XLA Ops:
  0.6 249.0 %shard_map.104 = (f32[9,16,16,256]{3,2,1,0:T(8,128)}, f32[3,16,16,256]{3,2,1,0:T(8,128)}) custom-call(f32[9,16,16,256]{3,2,1,0:T(8,128)} %state.1, s32[16,16,256]{2,1,0:T(8,128)} %region.1, f32[8]{0:T(128)} %lame.1, f32[8]{0:T(128)} %shear.1, f32[8]{0:T(128)} %buoyt.1, s32[1,1,32]{2,1,0:T(1,128)} %fblock.1, s32[1,1,32]{2,1,0:T(1,128)} %fowner.1, ...), custom_call_target="tpu_custom_call" | custom-call | tf_op jit(solution)/shard_map/pallas_call | solution.py:468
  249.7 0.0 copy-start
  249.7 3.3 %copy.13 = f32[9,16,16,256]{3,2,1,0:T(8,128)} copy(f32[9,16,16,256]{3,2,1,0:T(8,128)} %get-tuple-element.4) | data formatting | bytes 4718592
  253.0 0.0 copy-done
  253.0 0.9 copy.14
Async XLA Ops:
  249.7 3.4 %copy-start = (f32[3,16,16,256]{3,2,1,0:T(8,128)S(1)}, f32[3,16,16,256]{3,2,1,0:T(8,128)}, u32[]{:S(2)}) copy-start(f32[3,16,16,256]{3,2,1,0:T(8,128)} %get-tuple-element.5) | copy-start | bytes 2359300

commit v3 on v2

--- a/solution.py
+++ b/solution.py
@@ -62,15 +62,22 @@
 def kernel(
     state, region, lame, shear, buoyt, fblock, fowner, fslot, gain,
     out, sens_out,
-    V, S, own, dtb, sens, reg, bsend, brecv, csend, crecv, htab, onehot, rhs,
-    meta, mrecv, gtab, gs, srcv, srcs, bposv, bpos,
-    lsem, bs, br, cs, cr, zs, zr, ys, yr, ms, mr, hs, hr,
+    V, S, own, dtb, sens, reg, bsend, brecv, bloc, csend, crecv, htab, onehot, rhs,
+    meta, mrecv, gtab, gs, srcv, srcs, bposv, bpos, gvec, gland, gtwin,
+    lsem, bs, br, cs, cr, zs, zr, ys, yr, ms, mr, gsend, grecv, hs, hr,
 ):
     gz = lax.axis_index("gz")
     gy = lax.axis_index("gy")
     a0, b0, c0 = gz // 16, (gz // 4) % 4, gz % 4
     partners = [
         ((a0 + a) % 2) * 16 + ((b0 + b) % 4) * 4 + (c0 + c) % 4 for a, b, c in OFFSETS
+    ]
+    hh = gz % 16
+    near = [
+        (((b0 + b) % 4) * 4 + (c0 + c) % 4, b + c == 0) for b, c in sorted(
+            [(b, c) for b in range(4) for c in range(4)],
+            key=lambda o: -(min(o[0], 4 - o[0]) + min(o[1], 4 - o[1])),
+        )
     ]
     down, up = (gz + NGZ - 1) % NGZ, (gz + 1) % NGZ
     left, right = (gy + NGY - 1) % NGY, (gy + 1) % NGY
@@ -130,10 +137,12 @@
             for f in range(8):
                 S[f, l, xb, pl.ds(Y0, CY), :] = zero16
     for f in range(3):
-        csend[f, 0:8, :] = zero
-        csend[f, 64:72, :] = zero
         rhs[f, 192:256, :] = jnp.zeros((64, 384), BF16)
-    htab[32] = zero
+    htab[64] = zero
+    gains = jnp.zeros((8, LANE), F32)
+    for j in range(16):
+        gains = jnp.where(lax.broadcasted_iota(jnp.int32, (8, LANE), 1) == j, gain[0, 0, j], gains)
+    gvec[...] = gains
 
     lane8 = lax.broadcasted_iota(jnp.int32, (8, LANE), 1)
     lane_owner, lane_rank = lane8 % 32, (lane8 // 32) % 2
@@ -191,6 +200,8 @@
     for t in partners:
         meta_copy(t).start()
     mrecv[gz] = meta[...]
+    gcopy = remote(gvec, gland, gsend, grecv, ((gz + 16) % NGZ, gy))
+    gcopy.start()
 
     first = {
         "down": remote(S.at[3:8, 2:4, :, 14:30], S.at[3:8, 18:20, :, 14:30], hs.at[0], hr.at[0], (down, gy)),
@@ -224,21 +235,25 @@
     dev = lax.broadcasted_iota(jnp.int32, (NGZ, LANE), 0)
     got = mrecv[:, 1, :]
     gtab[...] = got
-    mine = (lane == gz) | (lane == gz + 32)
-    got = jnp.where(mine, got, -1)
-    place = 2 * dev + jnp.where(lane == gz + 32, 1, 0)
     lane1 = lax.broadcasted_iota(jnp.int32, (8, LANE), 1)
     acc = jnp.zeros((8, LANE), jnp.int32)
-    for s in range(32):
-        total = jnp.sum(jnp.where(got == s, place, 0))
-        acc = jnp.where(lane1 == s, total, acc)
-    srcv[...] = jnp.minimum(acc, POS - 1)
+    for e in range(2):
+        role = hh + 16 * e
+        of_role = jnp.where((lane == role) | (lane == role + 32), got, -1)
+        place = 4 * dev + 2 * e + jnp.where(lane == role + 32, 1, 0)
+        for s in range(32):
+            total = jnp.sum(jnp.where(of_role == s, place, 0))
+            acc = jnp.where((lane1 == s) & (sub == e), total, acc)
+    srcv[...] = jnp.clip(acc, 0, 4 * NGZ - 1)
+    gcopy.wait()
     c1 = pltpu.make_async_copy(gtab, gs, lsem.at[0, 0])
     c2 = pltpu.make_async_copy(srcv, srcs, lsem.at[0, 1])
     c3 = pltpu.make_async_copy(bposv, bpos, lsem.at[1, 0])
     c1.start()
     c2.start()
     c3.start()
+    c4 = pltpu.make_async_copy(gland, gtwin, lsem.at[1, 1])
+    c4.start()
 
     row = lax.broadcasted_iota(jnp.int32, (CY, LANE), 0)
     lane16 = lax.broadcasted_iota(jnp.int32, (CY, LANE), 1)
@@ -260,6 +275,7 @@
     c1.wait()
     c2.wait()
     c3.wait()
+    c4.wait()
     wait_send(first)
     wait_recv(first)
 
@@ -290,25 +306,21 @@
 
         lax.fori_loop(0, CZ, velocity, 0, unroll=4)
 
-        def pick(d, c):
-            for u in range(2):
-                b = bpos[0, u * 32 + d]
-                z, y, xb = b // 32, (b // 2) % 16, b % 2
-                for f in range(3):
-                    bsend[2 * d + u, pl.ds(f, 1), :] = own[f, z, xb, pl.ds(y, 1), :]
-            return c
-
-        lax.fori_loop(0, NGZ, pick, 0, unroll=8)
-
-        def b_copy(t):
-            return remote(
-                bsend.at[pl.ds(2 * t, 2), 0:3], brecv.at[pl.ds(2 * gz, 2), 0:3], bs, br, (t, gy)
-            )
-
-        for t in partners:
-            b_copy(t).start()
-        for u in range(2):
-            brecv[2 * gz + u] = bsend[2 * gz + u]
+        for t, here in near:
+            for e in range(2):
+                for u in range(2):
+                    b = bpos[0, u * 32 + e * 16 + t]
+                    z, y, xb = b // 32, (b // 2) % 16, b % 2
+                    for f in range(3):
+                        bsend[4 * t + 2 * e + u, pl.ds(f, 1), :] = own[f, z, xb, pl.ds(y, 1), :]
+            part = bsend.at[pl.ds(4 * t, 4), 0:3]
+            place = brecv.at[q, pl.ds(4 * gz, 4), 0:3]
+            remote(part, place, bs, br.at[q], (16 * (1 - a0) + t, gy)).start()
+            if here:
+                for u in range(4):
+                    brecv[q, 4 * gz + u] = bsend[4 * t + u]
+            else:
+                remote(part, place, bs, br.at[q], (16 * a0 + t, gy)).start()
 
         zc = {
             "down": remote(own.at[:, 0:3], V.at[q, :, 20:23, :, 14:30], zs.at[0], zr.at[q, 0], (down, gy)),
@@ -316,47 +328,55 @@
         }
         start(zc)
 
-        ball = brecv.at[0 : POS - 2, 0:3]
-        pltpu.make_async_copy(ball, ball, br).wait()
-
-        for j in range(16):
-            side0 = brecv[srcs[0, 2 * j]]
-            side1 = brecv[srcs[0, 2 * j + 1]]
-            slip = side0 - side1
-            traction = gain[0, 0, j] * slip / jnp.sqrt(1.0 + slip * slip)
-            htab[2 * j] = -0.5 * traction
-            htab[2 * j + 1] = 0.5 * traction
-
-        def reply(d, c):
-            for u in range(2):
-                slot = gs[d, u * 32 + gz]
-                slot = jnp.where((slot < 0) | (slot > 32), 32, slot)
-                for f in range(3):
-                    csend[f, pl.ds(2 * d + 2 + u, 1), :] = htab[slot, pl.ds(f, 1), :]
+        ball = brecv.at[q, 0 : 4 * (NGZ - 1), 0:3]
+        pltpu.make_async_copy(ball, ball, br.at[q]).wait()
+        for d in range(4 * NGZ):
+            bloc[d] = brecv[q, d]
+
+        for e in range(2):
+            for j in range(16):
+                side0 = bloc[srcs[e, 2 * j]]
+                side1 = bloc[srcs[e, 2 * j + 1]]
+                slip = side0 - side1
+                g = jnp.where(a0 == e, gain[0, 0, j], gtwin[0, j])
+                traction = g * slip / jnp.sqrt(1.0 + slip * slip)
+                htab[32 * e + 2 * j] = -0.5 * traction
+                htab[32 * e + 2 * j + 1] = 0.5 * traction
+
+        def reply(i, c):
+            d = jnp.clip(16 * a0 - 1 + i, 0, NGZ - 1)
+            for e in range(2):
+                for u in range(2):
+                    slot = gs[d, u * 32 + hh + 16 * e]
+                    slot = jnp.where((slot < 0) | (slot > 31), 64, slot + 32 * e)
+                    for f in range(3):
+                        csend[f, e, pl.ds(2 * i + u, 1), :] = htab[slot, pl.ds(f, 1), :]
             return c
 
-        lax.fori_loop(0, NGZ, reply, 0, unroll=8)
-
-        def c_copy(t):
-            return remote(csend.at[:, pl.ds(2 * t, 6)], crecv.at[:, pl.ds(6 * gz, 6)], cs, cr, (t, gy))
-
-        for t in partners:
-            c_copy(t).start()
-        for u in range(6):
-            for f in range(3):
-                crecv[f, pl.ds(6 * gz + u, 1), :] = csend[f, pl.ds(2 * gz + u, 1), :]
+        lax.fori_loop(0, 18, reply, 0, unroll=6)
+
+        for t, here in near:
+            if here:
+                for u in range(6):
+                    for f in range(3):
+                        for e in range(2):
+                            crecv[f, e, pl.ds(6 * hh + u, 1), :] = csend[f, e, pl.ds(2 * hh + u, 1), :]
+            else:
+                remote(
+                    csend.at[:, :, pl.ds(2 * t, 6)], crecv.at[:, :, pl.ds(6 * hh, 6)], cs, cr, (16 * a0 + t, gy)
+                ).start()
 
         pltpu.make_async_copy(ball, ball, bs).wait()
         wait_send(zc)
         wait_recv(zc)
-        call = crecv.at[:, 0 : 6 * (NGZ - 1)]
+        call = crecv.at[:, :, 0:90]
         pltpu.make_async_copy(call, call, cr).wait()
 
         for g in range(3):
             for f in range(3):
                 col = pl.ds(f * LANE, LANE)
                 d = jnp.concatenate(
-                    [crecv[f, pl.ds(2 * g + r, NGZ, stride=6), :] for r in range(2)], axis=0
+                    [crecv[f, e, pl.ds(2 * g + r, 16, stride=6), :] for r in range(2) for e in range(2)], axis=0
                 )
                 hi = d.astype(BF16)
                 d = d - hi.astype(F32)
@@ -387,8 +407,10 @@
         pltpu.make_async_copy(call, call, cs).wait()
 
         yc = {
-            "left": remote(V.at[q, :, 1:23, :, 14:17], V.at[q, :, 1:23, :, 30:33], ys.at[0], yr.at[q, 0], (gz, left)),
-            "right": remote(V.at[q, :, 1:23, :, 27:30], V.at[q, :, 1:23, :, 11:14], ys.at[1], yr.at[q, 1], (gz, right)),
+            "left2": remote(V.at[q, 1:3, 2:22, :, 14:17], V.at[q, 1:3, 2:22, :, 30:33], ys.at[2], yr.at[q, 2], (gz, left)),
+            "right2": remote(V.at[q, 1:3, 2:22, :, 27:30], V.at[q, 1:3, 2:22, :, 11:14], ys.at[3], yr.at[q, 3], (gz, right)),
+            "left": remote(V.at[q, 0, 4:20, :, 14:17], V.at[q, 0, 4:20, :, 30:33], ys.at[0], yr.at[q, 0], (gz, left)),
+            "right": remote(V.at[q, 0, 4:20, :, 27:30], V.at[q, 0, 4:20, :, 11:14], ys.at[1], yr.at[q, 1], (gz, right)),
         }
         start(yc)
 
@@ -481,10 +503,11 @@
             pltpu.VMEM((3, CZ, XB, CY, LANE), F32),
             pltpu.VMEM((CZ, XB, CY, LANE), jnp.int32),
             pltpu.VMEM((POS, 8, LANE), F32),
-            pltpu.VMEM((POS, 8, LANE), F32),
-            pltpu.VMEM((3, POS + 8, LANE), F32),
-            pltpu.VMEM((3, 6 * NGZ, LANE), F32),
-            pltpu.VMEM((33, 8, LANE), F32),
+            pltpu.VMEM((2, 4 * NGZ, 8, LANE), F32),
+            pltpu.VMEM((4 * NGZ, 8, LANE), F32),
+            pltpu.VMEM((3, 2, 40, LANE), F32),
+            pltpu.VMEM((3, 2, 96, LANE), F32),
+            pltpu.VMEM((65, 8, LANE), F32),
             pltpu.VMEM(((CZ + 6) * 32, 256), BF16),
             pltpu.VMEM((3, 256, 3 * LANE), BF16),
             pltpu.VMEM((8, LANE), jnp.int32),
@@ -495,15 +518,20 @@
             pltpu.SMEM((8, LANE), jnp.int32),
             pltpu.VMEM((8, LANE), jnp.int32),
             pltpu.SMEM((8, LANE), jnp.int32),
+            pltpu.VMEM((8, LANE), F32),
+            pltpu.VMEM((8, LANE), F32),
+            pltpu.SMEM((8, LANE), F32),
             dma((3, 2)),
             dma,
-            dma,
+            dma((2,)),
             dma,
             dma,
             dma((2,)),
             dma((2, 2)),
-            dma((2,)),
-            dma((2, 2)),
+            dma((4,)),
+            dma((2, 4)),
+            dma,
+            dma,
             dma,
             dma,
             dma((6,)),

time: 254 us -> 247 us (0.972)
  Pallas kernels: 249 us -> 242 us
    pallas_call x1, Pallas kernels: 249 us -> 242 us  [per_device(): pl.pallas_call(kernel, out_shape=(jax.ShapeDtypeStruct(state.shape, F32),...]
where the time goes in v3:
time: 247 us; the launch traced here: 246 us
  Pallas kernels  242 us (98%)
  local copies, waits for them, and re-layouts  4.23 us (2%)
    pallas_call x1, Pallas kernels, per_device(): pl.pallas_call(kernel, out_shape=(jax.ShapeDtypeStruct(state.shape, F32),...  242 us

profile of v3, /device:TPU:1, one launch (start us, length us, event | category | flops | bytes accessed | tf_op | source)
XLA Modules:
  0.0 246.4 jit_solution(13068168861816622963)
XLA Ops:
  0.6 241.6 %shard_map.104 = (f32[9,16,16,256]{3,2,1,0:T(8,128)}, f32[3,16,16,256]{3,2,1,0:T(8,128)}) custom-call(f32[9,16,16,256]{3,2,1,0:T(8,128)} %state.1, s32[16,16,256]{2,1,0:T(8,128)} %region.1, f32[8]{0:T(128)} %lame.1, f32[8]{0:T(128)} %shear.1, f32[8]{0:T(128)} %buoyt.1, s32[1,1,32]{2,1,0:T(1,128)} %fblock.1, s32[1,1,32]{2,1,0:T(1,128)} %fowner.1, ...), custom_call_target="tpu_custom_call" | custom-call | tf_op jit(solution)/shard_map/pallas_call | solution.py:490
  242.2 0.0 copy-start
  242.2 3.3 %copy.13 = f32[9,16,16,256]{3,2,1,0:T(8,128)} copy(f32[9,16,16,256]{3,2,1,0:T(8,128)} %get-tuple-element.4) | data formatting | bytes 4718592
  245.6 0.0 copy-done
  245.6 0.9 copy.14
Async XLA Ops:
  242.2 3.4 %copy-start = (f32[3,16,16,256]{3,2,1,0:T(8,128)S(1)}, f32[3,16,16,256]{3,2,1,0:T(8,128)}, u32[]{:S(2)}) copy-start(f32[3,16,16,256]{3,2,1,0:T(8,128)} %get-tuple-element.5) | copy-start | bytes 2359300

commit v4 on v3

--- a/solution.py
+++ b/solution.py
@@ -372,7 +372,7 @@
         call = crecv.at[:, :, 0:90]
         pltpu.make_async_copy(call, call, cr).wait()
 
-        for g in range(3):
+        def terms(g):
             for f in range(3):
                 col = pl.ds(f * LANE, LANE)
                 d = jnp.concatenate(
@@ -400,19 +400,32 @@
                             here + delta[r : r + 16, f * LANE : (f + 1) * LANE]
                         )
 
+        def strips(part, fields, layers):
+            low, high = V.at[q, fields, layers, :, 14:17], V.at[q, fields, layers, :, 27:30]
+            after, before = V.at[q, fields, layers, :, 30:33], V.at[q, fields, layers, :, 11:14]
+            return {
+                "left": remote(low, after, ys.at[0, part], yr.at[q, 0, part], (gz, left)),
+                "right": remote(high, before, ys.at[1, part], yr.at[q, 1, part], (gz, right)),
+            }
+
+        yc = [
+            strips(0, slice(0, 3), slice(4, 12)),
+            strips(1, slice(0, 3), slice(12, 20)),
+            strips(2, slice(1, 3), slice(2, 4)),
+            strips(3, slice(1, 3), slice(20, 22)),
+        ]
+        terms(1)
+        apply(3, 8, 1)
+        start(yc[0])
+        apply(11, 8, 1)
+        start(yc[1])
+        terms(0)
         apply(0, 3, 0)
+        start(yc[2])
+        terms(2)
         apply(19, 3, 2)
-        apply(3, 8, 1)
-        apply(11, 8, 1)
+        start(yc[3])
         pltpu.make_async_copy(call, call, cs).wait()
-
-        yc = {
-            "left2": remote(V.at[q, 1:3, 2:22, :, 14:17], V.at[q, 1:3, 2:22, :, 30:33], ys.at[2], yr.at[q, 2], (gz, left)),
-            "right2": remote(V.at[q, 1:3, 2:22, :, 27:30], V.at[q, 1:3, 2:22, :, 11:14], ys.at[3], yr.at[q, 3], (gz, right)),
-            "left": remote(V.at[q, 0, 4:20, :, 14:17], V.at[q, 0, 4:20, :, 30:33], ys.at[0], yr.at[q, 0], (gz, left)),
-            "right": remote(V.at[q, 0, 4:20, :, 27:30], V.at[q, 0, 4:20, :, 11:14], ys.at[1], yr.at[q, 1], (gz, right)),
-        }
-        start(yc)
 
         def sensitivity(k, c):
             for f in range(3):
@@ -454,8 +467,9 @@
             return c
 
         lax.fori_loop(0, SZ, functools.partial(stress, (1,)), 0, unroll=5)
-        wait_send(yc)
-        wait_recv(yc)
+        for part in yc:
+            wait_send(part)
+            wait_recv(part)
         lax.fori_loop(0, SZ, functools.partial(stress, (0, 2)), 0, unroll=4)
         return carry
 
@@ -528,8 +542,8 @@
             dma,
             dma((2,)),
             dma((2, 2)),
-            dma((4,)),
             dma((2, 4)),
+            dma((2, 2, 4)),
             dma,
             dma,
             dma,

time: 247 us -> 246 us (level)
  no operation moved by 1% of the time
where the time goes in v4:
time: 246 us
  Pallas kernels  241 us (98%)
  local copies, waits for them, and re-layouts  4.23 us (2%)
    pallas_call x1, Pallas kernels, per_device(): pl.pallas_call(kernel, out_shape=(jax.ShapeDtypeStruct(state.shape, F32),...  241 us

profile of v4, /device:TPU:1, one launch (start us, length us, event | category | flops | bytes accessed | tf_op | source)
XLA Modules:
  0.0 246.3 jit_solution(13406764065262675643)
XLA Ops:
  0.6 241.4 %shard_map.104 = (f32[9,16,16,256]{3,2,1,0:T(8,128)}, f32[3,16,16,256]{3,2,1,0:T(8,128)}) custom-call(f32[9,16,16,256]{3,2,1,0:T(8,128)} %state.1, s32[16,16,256]{2,1,0:T(8,128)} %region.1, f32[8]{0:T(128)} %lame.1, f32[8]{0:T(128)} %shear.1, f32[8]{0:T(128)} %buoyt.1, s32[1,1,32]{2,1,0:T(1,128)} %fblock.1, s32[1,1,32]{2,1,0:T(1,128)} %fowner.1, ...), custom_call_target="tpu_custom_call" | custom-call | tf_op jit(solution)/shard_map/pallas_call | solution.py:504
  242.1 0.0 copy-start
  242.1 3.3 %copy.13 = f32[9,16,16,256]{3,2,1,0:T(8,128)} copy(f32[9,16,16,256]{3,2,1,0:T(8,128)} %get-tuple-element.4) | data formatting | bytes 4718592
  245.4 0.0 copy-done
  245.4 0.9 copy.14
Async XLA Ops:
  242.1 3.4 %copy-start = (f32[3,16,16,256]{3,2,1,0:T(8,128)S(1)}, f32[3,16,16,256]{3,2,1,0:T(8,128)}, u32[]{:S(2)}) copy-start(f32[3,16,16,256]{3,2,1,0:T(8,128)} %get-tuple-element.5) | copy-start | bytes 2359300

commit v5 on v4

--- a/solution.py
+++ b/solution.py
@@ -367,8 +367,6 @@
                 ).start()
 
         pltpu.make_async_copy(ball, ball, bs).wait()
-        wait_send(zc)
-        wait_recv(zc)
         call = crecv.at[:, :, 0:90]
         pltpu.make_async_copy(call, call, cr).wait()
 
@@ -419,6 +417,8 @@
         start(yc[0])
         apply(11, 8, 1)
         start(yc[1])
+        wait_send(zc)
+        wait_recv(zc)
         terms(0)
         apply(0, 3, 0)
         start(yc[2])

time: 246 us -> 248 us (level)
  no operation moved by 1% of the time
where the time goes in v5:
time: 248 us
  Pallas kernels  243 us (98%)
  local copies, waits for them, and re-layouts  4.23 us (2%)
    pallas_call x1, Pallas kernels, per_device(): pl.pallas_call(kernel, out_shape=(jax.ShapeDtypeStruct(state.shape, F32),...  243 us

profile of v5, /device:TPU:1, one launch (start us, length us, event | category | flops | bytes accessed | tf_op | source)
XLA Modules:
  0.0 248.3 jit_solution(2377018344989768406)
XLA Ops:
  0.6 243.4 %shard_map.104 = (f32[9,16,16,256]{3,2,1,0:T(8,128)}, f32[3,16,16,256]{3,2,1,0:T(8,128)}) custom-call(f32[9,16,16,256]{3,2,1,0:T(8,128)} %state.1, s32[16,16,256]{2,1,0:T(8,128)} %region.1, f32[8]{0:T(128)} %lame.1, f32[8]{0:T(128)} %shear.1, f32[8]{0:T(128)} %buoyt.1, s32[1,1,32]{2,1,0:T(1,128)} %fblock.1, s32[1,1,32]{2,1,0:T(1,128)} %fowner.1, ...), custom_call_target="tpu_custom_call" | custom-call | tf_op jit(solution)/shard_map/pallas_call | solution.py:504
  244.0 0.0 copy-start
  244.0 3.3 %copy.13 = f32[9,16,16,256]{3,2,1,0:T(8,128)} copy(f32[9,16,16,256]{3,2,1,0:T(8,128)} %get-tuple-element.4) | data formatting | bytes 4718592
  247.4 0.0 copy-done
  247.4 0.9 copy.14
Async XLA Ops:
  244.0 3.4 %copy-start = (f32[3,16,16,256]{3,2,1,0:T(8,128)S(1)}, f32[3,16,16,256]{3,2,1,0:T(8,128)}, u32[]{:S(2)}) copy-start(f32[3,16,16,256]{3,2,1,0:T(8,128)} %get-tuple-element.5) | copy-start | bytes 2359300
